TPU v7x, 128 devices: a whole 4x4x4 slice. The times are simulated.
128 devices in a mesh: ctx: 16 (over y, x_hi, core), wt: 8 (over x_lo, z).
Axes of the slice: x: 4 (x_hi: 2, x_lo: 2; x = x_hi * 2 + x_lo), y: 4, z: 4, core: 2. Of those that a mesh axis runs over, the one named last changes fastest.
Arguments:
- inputs: bfloat16 [8, 4096, 512], P('wt', 'ctx'), may hold values from -6 to 6
- lengths: int32 [8], P('wt'), may hold values from 1024 to 4096, as said below
- cotangent: bfloat16 [8, 4096, 512], P('wt', 'ctx'), may hold values from -6 to 6
- glu_gain: bfloat16 [512], P('wt'), may hold values from 0.5 to 1.5
- glu_value: bfloat16 [512, 512], P('wt'), may hold values from -0.25 to 0.25
- glu_gate: bfloat16 [512, 512], P('wt'), may hold values from -0.25 to 0.25
- conv_gain: bfloat16 [512], P('wt'), may hold values from 0.5 to 1.5
- wide_weight: bfloat16 [512, 2048], P('wt'), may hold values from -0.25 to 0.25
- narrow_weight: bfloat16 [3, 512, 256], P(None, 'wt'), may hold values from -0.15625 to 0.15625
- mid_gain: bfloat16 [2048], P('wt'), may hold values from 0.5 to 1.5
- depth_weight: bfloat16 [9, 2048], P(None, 'wt'), may hold values from -2 to 2
- point_weight: bfloat16 [2048, 256], P('wt'), may hold values from -0.125 to 0.125
- attn_gain: bfloat16 [512], P('wt'), may hold values from 0.5 to 1.5
- query_weight: bfloat16 [512, 512], P('wt'), may hold values from -0.5 to 0.5
- key_weight: bfloat16 [512, 512], P('wt'), may hold values from -0.25 to 0.25
- value_weight: bfloat16 [512, 512], P('wt'), may hold values from -0.25 to 0.25
- output_weight: bfloat16 [512, 512], P('wt'), may hold values from -1.5 to 1.5
- ffn_gain: bfloat16 [512], P('wt'), may hold values from 0.5 to 1.5
- ffn_in: bfloat16 [512, 2048], P('wt'), may hold values from -0.25 to 0.25
- ffn_out: bfloat16 [2048, 512], P('wt'), may hold values from -0.125 to 0.125
Outputs:
- output: bfloat16 [8, 4096, 512], P('wt', 'ctx')
- input_grad: float32 [8, 4096, 512], P('wt', 'ctx')
- grad_glu_gain: float32 [512], P('wt')
- grad_glu_value: float32 [512, 512], P('wt')
- grad_glu_gate: float32 [512, 512], P('wt')
- grad_conv_gain: float32 [512], P('wt')
- grad_wide_weight: float32 [512, 2048], P('wt')
- grad_narrow_weight: float32 [3, 512, 256], P(None, 'wt')
- grad_mid_gain: float32 [2048], P('wt')
- grad_depth_weight: float32 [9, 2048], P(None, 'wt')
- grad_point_weight: float32 [2048, 256], P('wt')
- grad_attn_gain: float32 [512], P('wt')
- grad_query_weight: float32 [512, 512], P('wt')
- grad_key_weight: float32 [512, 512], P('wt')
- grad_value_weight: float32 [512, 512], P('wt')
- grad_output_weight: float32 [512, 512], P('wt')
- grad_ffn_gain: float32 [512], P('wt')
- grad_ffn_in: float32 [512, 2048], P('wt')
- grad_ffn_out: float32 [2048, 512], P('wt')
Inputs may be any that keep to these rules, and one draw needn't show every extreme that they name: `lengths`: valid slots of each sequence, which are its first slots; one sequence has exactly 4096 and one exactly 1024.
All inputs are finite; a program needn't handle non-finite values.
Results may differ from a plain program's by a relative error of at most 0.03.
Values may be sent and summed in bfloat16 or wider, within the bound.
No kernel may reach another device: no remote copies, remote signals or barrier semaphores. Data moves between devices by JAX's collectives and lax.ppermute only.
A program may use at most 256 MiB of HBM per device.

v0:
```python
import jax
import jax.numpy as jnp
from jax import lax
from jax.sharding import PartitionSpec as P

HEADS = 8
HEAD = 64
EPSILON = 1e-06


def with_halo(block, sides, width):
    for axis, dim in sides:
        count = lax.axis_size(axis)
        forward = [(i, i + 1) for i in range(count - 1)]
        backward = [(target, source) for source, target in forward]
        low = lax.ppermute(
            lax.slice_in_dim(block, block.shape[dim] - width, None, axis=dim), axis, forward
        )
        high = lax.ppermute(lax.slice_in_dim(block, 0, width, axis=dim), axis, backward)
        block = jnp.concatenate([low, block, high], axis=dim)
    return block


def matmul(left, right):
    return jnp.dot(left, right, preferred_element_type=jnp.float32)


def inner_rows(left, right):
    return lax.dot_general(
        left, right, (((0,), (0,)), ((), ())), preferred_element_type=jnp.float32
    )


def outer_cols(left, right):
    return lax.dot_general(
        left, right, (((1,), (1,)), ((), ())), preferred_element_type=jnp.float32
    )


def smooth_unit(value):
    return value * jax.nn.sigmoid(value)


def smooth_slope(value):
    sigma = jax.nn.sigmoid(value)
    return sigma * (1.0 + value * (1.0 - sigma))


def layer_norm(value, gain):
    average = jnp.mean(value, -1, keepdims=True)
    centred = value - average
    scale = lax.rsqrt(jnp.mean(centred * centred, -1, keepdims=True) + EPSILON)
    normal = centred * scale
    return (normal * gain.astype(jnp.float32), normal, scale)


def norm_back(incoming, normal, scale, gain):
    scaled = incoming * gain.astype(jnp.float32)
    gain_grad = jnp.sum(incoming * normal, 0)
    value_grad = scale * (
        scaled
        - jnp.mean(scaled, -1, keepdims=True)
        - normal * jnp.mean(scaled * normal, -1, keepdims=True)
    )
    return (value_grad, gain_grad)


def edges_forward(values, reach):
    return with_halo(values, (("ctx", 0),), reach)


def edges_backward(values, reach):
    return with_halo(values, (("ctx", 0),), reach)


def head_scores(queries, keys, key_valid, factor):
    logits = outer_cols(queries, keys) * factor
    return jnp.where(key_valid[None, :], logits, -1e30)


def shards(
    inputs,
    lengths,
    cotangent,
    glu_gain,
    glu_value,
    glu_gate,
    conv_gain,
    wide_weight,
    narrow_weight,
    mid_gain,
    depth_weight,
    point_weight,
    attn_gain,
    query_weight,
    key_weight,
    value_weight,
    output_weight,
    ffn_gain,
    ffn_in,
    ffn_out,
):
    rows = inputs.shape[1]
    width = inputs.shape[2]
    half = narrow_weight.shape[2]
    units = wide_weight.shape[1]
    total_rows = rows * lax.axis_size("ctx")
    factor = HEAD ** (-0.5)
    positions = lax.axis_index("ctx") * rows + jnp.arange(rows, dtype=jnp.int32)
    local_valid = positions < lengths[0]
    valid = local_valid.astype(jnp.float32)[:, None]
    key_valid = jnp.arange(total_rows, dtype=jnp.int32) < lengths[0]
    hidden = inputs[0].astype(jnp.float32)
    g_glu, w_val, w_gat = (
        lax.all_gather(glu_gain, "wt", axis=0, tiled=True),
        lax.all_gather(glu_value, "wt", axis=0, tiled=True),
        lax.all_gather(glu_gate, "wt", axis=0, tiled=True),
    )
    normed, glu_hat, glu_scale = layer_norm(hidden, g_glu)
    glu_in = normed.astype(jnp.bfloat16)
    value_part = matmul(glu_in, w_val)
    gate_part = matmul(glu_in, w_gat)
    sigma = jax.nn.sigmoid(gate_part)
    after_glu = hidden + value_part * sigma
    g_conv, w_wid, w_nar, g_mid, w_dep, w_pnt = (
        lax.all_gather(conv_gain, "wt", axis=0, tiled=True),
        lax.all_gather(wide_weight, "wt", axis=0, tiled=True),
        lax.all_gather(narrow_weight, "wt", axis=1, tiled=True),
        lax.all_gather(mid_gain, "wt", axis=0, tiled=True),
        lax.all_gather(depth_weight, "wt", axis=1, tiled=True),
        lax.all_gather(point_weight, "wt", axis=0, tiled=True),
    )
    normed, conv_hat, conv_scale = layer_norm(after_glu, g_conv)
    conv_in = (normed * valid).astype(jnp.bfloat16)
    wide_pre = matmul(conv_in, w_wid)
    conv_rim = edges_forward(conv_in, 1)
    stacked = jnp.concatenate(
        [conv_rim[0:rows], conv_rim[1 : rows + 1], conv_rim[2 : rows + 2]], axis=1
    )
    narrow_pre = matmul(stacked, w_nar.reshape(3 * width, half))
    mixed = smooth_unit(wide_pre) + jnp.pad(smooth_unit(narrow_pre), ((0, 0), (0, units - half)))
    normed, mid_hat, mid_scale = layer_norm(mixed, g_mid)
    mid_in = (normed * valid).astype(jnp.bfloat16)
    mid_rim = edges_forward(mid_in, 4)
    depth_float = w_dep.astype(jnp.float32)
    spread = sum(
        (mid_rim[tap : tap + rows].astype(jnp.float32) * depth_float[tap] for tap in range(9))
    )
    spread_in = spread.astype(jnp.bfloat16)
    separable = matmul(spread_in, w_pnt)
    after_conv = after_glu + jnp.pad(separable, ((0, 0), (0, width - half)))
    g_att, w_qry, w_key, w_vls, w_outp = (
        lax.all_gather(attn_gain, "wt", axis=0, tiled=True),
        lax.all_gather(query_weight, "wt", axis=0, tiled=True),
        lax.all_gather(key_weight, "wt", axis=0, tiled=True),
        lax.all_gather(value_weight, "wt", axis=0, tiled=True),
        lax.all_gather(output_weight, "wt", axis=0, tiled=True),
    )
    normed, attn_hat, attn_scale = layer_norm(after_conv, g_att)
    attn_in = normed.astype(jnp.bfloat16)
    queries = matmul(attn_in, w_qry).astype(jnp.bfloat16)
    keys_local = matmul(attn_in, w_key).astype(jnp.bfloat16)
    values_local = matmul(attn_in, w_vls).astype(jnp.bfloat16)
    keys_all, values_all = (
        lax.all_gather(keys_local, "ctx", axis=0, tiled=True),
        lax.all_gather(values_local, "ctx", axis=0, tiled=True),
    )
    head_outs = []
    head_lse = []
    for head_index in range(HEADS):
        cols = slice(head_index * HEAD, (head_index + 1) * HEAD)
        logits = head_scores(queries[:, cols], keys_all[:, cols], key_valid, factor)
        highest = jnp.max(logits, -1, keepdims=True)
        expo = jnp.exp(logits - highest)
        totals = jnp.sum(expo, -1, keepdims=True)
        probs = (expo / totals).astype(jnp.bfloat16)
        head_outs.append(matmul(probs, values_all[:, cols]))
        head_lse.append(highest + jnp.log(totals))
    heads_in = jnp.concatenate(head_outs, 1).astype(jnp.bfloat16)
    after_attn = after_conv + matmul(heads_in, w_outp)
    g_ffn, w_upper, w_lower = (
        lax.all_gather(ffn_gain, "wt", axis=0, tiled=True),
        lax.all_gather(ffn_in, "wt", axis=0, tiled=True),
        lax.all_gather(ffn_out, "wt", axis=0, tiled=True),
    )
    normed, ffn_hat, ffn_scale = layer_norm(after_attn, g_ffn)
    ffn_input = normed.astype(jnp.bfloat16)
    ffn_pre = matmul(ffn_input, w_upper)
    activated = smooth_unit(ffn_pre).astype(jnp.bfloat16)
    result = (after_attn + matmul(activated, w_lower)) * valid
    grad = cotangent[0].astype(jnp.float32) * valid
    grad_low = grad.astype(jnp.bfloat16)
    d_lower = inner_rows(activated, grad_low)
    d_pre = (outer_cols(grad_low, w_lower) * smooth_slope(ffn_pre)).astype(jnp.bfloat16)
    d_upper = inner_rows(ffn_input, d_pre)
    back, d_gffn = norm_back(outer_cols(d_pre, w_upper), ffn_hat, ffn_scale, g_ffn)
    grad = grad + back
    s_gffn, s_upper, s_lower = (
        lax.psum_scatter(d_gffn.astype(jnp.bfloat16), "wt", scatter_dimension=0, tiled=True).astype(
            jnp.float32
        ),
        lax.psum_scatter(
            d_upper.astype(jnp.bfloat16), "wt", scatter_dimension=0, tiled=True
        ).astype(jnp.float32),
        lax.psum_scatter(
            d_lower.astype(jnp.bfloat16), "wt", scatter_dimension=0, tiled=True
        ).astype(jnp.float32),
    )
    grad_low = grad.astype(jnp.bfloat16)
    d_outp = inner_rows(heads_in, grad_low)
    d_heads = outer_cols(grad_low, w_outp).astype(jnp.bfloat16)
    keys_back, values_back = (
        lax.all_gather(keys_local, "ctx", axis=0, tiled=True),
        lax.all_gather(values_local, "ctx", axis=0, tiled=True),
    )
    query_grads = []
    key_grads = []
    value_grads = []
    row_sums = []
    for head_index in range(HEADS):
        cols = slice(head_index * HEAD, (head_index + 1) * HEAD)
        logits = head_scores(queries[:, cols], keys_back[:, cols], key_valid, factor)
        probs_full = jnp.exp(logits - head_lse[head_index])
        d_probs = outer_cols(d_heads[:, cols], values_back[:, cols])
        row_total = jnp.sum(probs_full * d_probs, -1, keepdims=True)
        row_sums.append(row_total)
        d_scores = (probs_full * (d_probs - row_total)).astype(jnp.bfloat16)
        query_grads.append(matmul(d_scores, keys_back[:, cols]) * factor)
        probs = probs_full.astype(jnp.bfloat16)
        key_grads.append(inner_rows(d_scores, queries[:, cols]) * factor)
        value_grads.append(inner_rows(probs, d_heads[:, cols]))
    d_keys, d_values = (
        lax.psum_scatter(
            jnp.concatenate(key_grads, 1).astype(jnp.bfloat16),
            "ctx",
            scatter_dimension=0,
            tiled=True,
        ).astype(jnp.float32),
        lax.psum_scatter(
            jnp.concatenate(value_grads, 1).astype(jnp.bfloat16),
            "ctx",
            scatter_dimension=0,
            tiled=True,
        ).astype(jnp.float32),
    )
    dq_low = jnp.concatenate(query_grads, 1).astype(jnp.bfloat16)
    dk_low = d_keys.astype(jnp.bfloat16)
    dv_low = d_values.astype(jnp.bfloat16)
    d_qry = inner_rows(attn_in, dq_low)
    d_key = inner_rows(attn_in, dk_low)
    d_vls = inner_rows(attn_in, dv_low)
    d_norm = outer_cols(dq_low, w_qry) + outer_cols(dk_low, w_key) + outer_cols(dv_low, w_vls)
    back, d_gatt = norm_back(d_norm, attn_hat, attn_scale, g_att)
    grad = grad + back
    s_gatt, s_qry, s_key, s_vls, s_outp = (
        lax.psum_scatter(d_gatt.astype(jnp.bfloat16), "wt", scatter_dimension=0, tiled=True).astype(
            jnp.float32
        ),
        lax.psum_scatter(d_qry.astype(jnp.bfloat16), "wt", scatter_dimension=0, tiled=True).astype(
            jnp.float32
        ),
        lax.psum_scatter(d_key.astype(jnp.bfloat16), "wt", scatter_dimension=0, tiled=True).astype(
            jnp.float32
        ),
        lax.psum_scatter(d_vls.astype(jnp.bfloat16), "wt", scatter_dimension=0, tiled=True).astype(
            jnp.float32
        ),
        lax.psum_scatter(d_outp.astype(jnp.bfloat16), "wt", scatter_dimension=0, tiled=True).astype(
            jnp.float32
        ),
    )
    sep_grad = grad[:, :half].astype(jnp.bfloat16)
    d_pnt = inner_rows(spread_in, sep_grad)
    d_spread = outer_cols(sep_grad, w_pnt).astype(jnp.bfloat16)
    spread_float = d_spread.astype(jnp.float32)
    d_dep = jnp.stack(
        [
            jnp.sum(mid_rim[tap : tap + rows].astype(jnp.float32) * spread_float, 0)
            for tap in range(9)
        ]
    )
    spread_rim = edges_backward(d_spread, 4)
    d_mid = sum(
        (
            spread_rim[8 - tap : 8 - tap + rows].astype(jnp.float32) * depth_float[tap]
            for tap in range(9)
        )
    )
    back_mid, d_gmid = norm_back(d_mid * valid, mid_hat, mid_scale, g_mid)
    d_wide_pre = (back_mid * smooth_slope(wide_pre)).astype(jnp.bfloat16)
    d_nar_pre = (back_mid[:, :half] * smooth_slope(narrow_pre)).astype(jnp.bfloat16)
    d_wid = inner_rows(conv_in, d_wide_pre)
    d_nar = inner_rows(stacked, d_nar_pre).reshape(3, width, half)
    nar_rim = edges_backward(d_nar_pre, 1)
    back_stack = jnp.concatenate(
        [nar_rim[2 : rows + 2], nar_rim[1 : rows + 1], nar_rim[0:rows]], axis=1
    )
    d_conv = outer_cols(d_wide_pre, w_wid) + outer_cols(
        back_stack, w_nar.transpose(1, 0, 2).reshape(width, 3 * half)
    )
    back, d_gconv = norm_back(d_conv * valid, conv_hat, conv_scale, g_conv)
    grad = grad + back
    s_gconv, s_wid, s_nar, s_gmid, s_dep, s_pnt = (
        lax.psum_scatter(
            d_gconv.astype(jnp.bfloat16), "wt", scatter_dimension=0, tiled=True
        ).astype(jnp.float32),
        lax.psum_scatter(d_wid.astype(jnp.bfloat16), "wt", scatter_dimension=0, tiled=True).astype(
            jnp.float32
        ),
        lax.psum_scatter(d_nar.astype(jnp.bfloat16), "wt", scatter_dimension=1, tiled=True).astype(
            jnp.float32
        ),
        lax.psum_scatter(d_gmid.astype(jnp.bfloat16), "wt", scatter_dimension=0, tiled=True).astype(
            jnp.float32
        ),
        lax.psum_scatter(d_dep.astype(jnp.bfloat16), "wt", scatter_dimension=1, tiled=True).astype(
            jnp.float32
        ),
        lax.psum_scatter(d_pnt.astype(jnp.bfloat16), "wt", scatter_dimension=0, tiled=True).astype(
            jnp.float32
        ),
    )
    d_value = (grad * sigma).astype(jnp.bfloat16)
    d_gate = (grad * value_part * sigma * (1.0 - sigma)).astype(jnp.bfloat16)
    d_wval = inner_rows(glu_in, d_value)
    d_wgat = inner_rows(glu_in, d_gate)
    d_norm = outer_cols(d_value, w_val) + outer_cols(d_gate, w_gat)
    back, d_gglu = norm_back(d_norm, glu_hat, glu_scale, g_glu)
    grad = grad + back
    s_gglu, s_wval, s_wgat = (
        lax.psum_scatter(d_gglu.astype(jnp.bfloat16), "wt", scatter_dimension=0, tiled=True).astype(
            jnp.float32
        ),
        lax.psum_scatter(d_wval.astype(jnp.bfloat16), "wt", scatter_dimension=0, tiled=True).astype(
            jnp.float32
        ),
        lax.psum_scatter(d_wgat.astype(jnp.bfloat16), "wt", scatter_dimension=0, tiled=True).astype(
            jnp.float32
        ),
    )
    summed = (
        lax.psum(s_gglu.astype(jnp.bfloat16), "ctx").astype(jnp.float32),
        lax.psum(s_wval.astype(jnp.bfloat16), "ctx").astype(jnp.float32),
        lax.psum(s_wgat.astype(jnp.bfloat16), "ctx").astype(jnp.float32),
        lax.psum(s_gconv.astype(jnp.bfloat16), "ctx").astype(jnp.float32),
        lax.psum(s_wid.astype(jnp.bfloat16), "ctx").astype(jnp.float32),
        lax.psum(s_nar.astype(jnp.bfloat16), "ctx").astype(jnp.float32),
        lax.psum(s_gmid.astype(jnp.bfloat16), "ctx").astype(jnp.float32),
        lax.psum(s_dep.astype(jnp.bfloat16), "ctx").astype(jnp.float32),
        lax.psum(s_pnt.astype(jnp.bfloat16), "ctx").astype(jnp.float32),
        lax.psum(s_gatt.astype(jnp.bfloat16), "ctx").astype(jnp.float32),
        lax.psum(s_qry.astype(jnp.bfloat16), "ctx").astype(jnp.float32),
        lax.psum(s_key.astype(jnp.bfloat16), "ctx").astype(jnp.float32),
        lax.psum(s_vls.astype(jnp.bfloat16), "ctx").astype(jnp.float32),
        lax.psum(s_outp.astype(jnp.bfloat16), "ctx").astype(jnp.float32),
        lax.psum(s_gffn.astype(jnp.bfloat16), "ctx").astype(jnp.float32),
        lax.psum(s_upper.astype(jnp.bfloat16), "ctx").astype(jnp.float32),
        lax.psum(s_lower.astype(jnp.bfloat16), "ctx").astype(jnp.float32),
    )
    return (result.astype(jnp.bfloat16)[None], grad[None]) + tuple(summed)


def solution(mesh):
    return jax.shard_map(
        shards,
        mesh=mesh,
        in_specs=(
            P("wt", "ctx", None),
            P("wt"),
            P("wt", "ctx", None),
            P("wt"),
            P("wt", None),
            P("wt", None),
            P("wt"),
            P("wt", None),
            P(None, "wt", None),
            P("wt"),
            P(None, "wt"),
            P("wt", None),
            P("wt"),
            P("wt", None),
            P("wt", None),
            P("wt", None),
            P("wt", None),
            P("wt"),
            P("wt", None),
            P("wt", None),
        ),
        out_specs=(
            P("wt", "ctx", None),
            P("wt", "ctx", None),
            P("wt"),
            P("wt", None),
            P("wt", None),
            P("wt"),
            P("wt", None),
            P(None, "wt", None),
            P("wt"),
            P(None, "wt"),
            P("wt", None),
            P("wt"),
            P("wt", None),
            P("wt", None),
            P("wt", None),
            P("wt", None),
            P("wt"),
            P("wt", None),
            P("wt", None),
        ),
        check_vma=False,
    )
```

profile of v0, /device:TPU:0, one launch (start us, length us, event | category | flops | bytes accessed | tf_op | source)
XLA Modules:
  0.0 1289.7 jit_solution(4152932484720257702)
XLA Ops:
  14.0 21.1 %all-reduce.14 = (bf16[512]{0:T(512)(128)(2,1)S(1)}, bf16[512]{0:T(512)(128)(2,1)S(1)}, bf16[512]{0:T(512)(128)(2,1)S(1)}, bf16[512]{0:T(512)(128)(2,1)S(1)}) all-reduce(bf16[512]{0:T(512)(128)(2,1)S(1)} %dynamic-update-slice, bf16[512]{0:T(512)(128)(2,1)S(1)} %dynamic-update-slice.1, ...), channel_id=1, replica_groups=mesh['ctx'=16,'wt'=8] {'wt'}, use_global_device_ids=true, to_apply=%add.2 | all-reduce | flops 2048 | bytes 8192
  37.4 29.6 %all_gather.60 = bf16[512,512]{1,0:T(8,128)(2,1)S(1)} all-gather(bf16[64,512]{1,0:T(8,128)(2,1)} %param.24), channel_id=1, replica_groups=mesh['ctx'=16,'wt'=8] {'wt'}, dimensions={0}, use_global_device_ids=true | all-gather | bytes 589824 | tf_op jit(solution)/shard_map/all_gather | solution.py:116
  67.0 29.2 %all_gather.61 = bf16[512,512]{1,0:T(8,128)(2,1)S(1)} all-gather(bf16[64,512]{1,0:T(8,128)(2,1)} %param.25), channel_id=1, replica_groups=mesh['ctx'=16,'wt'=8] {'wt'}, dimensions={0}, use_global_device_ids=true | all-gather | bytes 589824 | tf_op jit(solution)/shard_map/all_gather | solution.py:117
  102.8 28.2 %all_gather.66 = bf16[9,2048]{1,0:T(8,128)(2,1)S(1)} all-gather(bf16[9,256]{1,0:T(8,128)(2,1)S(1)} %copy-done.142), channel_id=1, replica_groups=mesh['ctx'=16,'wt'=8] {'wt'}, dimensions={1}, use_global_device_ids=true | all-gather | bytes 41472 | tf_op jit(solution)/shard_map/all_gather | solution.py:130
  131.2 29.7 %all_gather.64 = bf16[3,512,256]{2,1,0:T(8,128)(2,1)S(1)} all-gather(bf16[3,64,256]{2,1,0:T(8,128)(2,1)S(1)} %copy-done.98), channel_id=1, replica_groups=mesh['ctx'=16,'wt'=8] {'wt'}, dimensions={1}, use_global_device_ids=true | all-gather | bytes 884736 | tf_op jit(solution)/shard_map/all_gather | solution.py:128
  160.9 16.3 %all-gather = bf16[8,1,256]{2,1,0:T(2,128)(2,1)S(1)} all-gather(bf16[1,1,256]{2,1,0:T(2,128)(2,1)S(1)} %reshape.267), channel_id=1, replica_groups=mesh['ctx'=16,'wt'=8] {'wt'}, dimensions={0}, use_global_device_ids=true | all-gather | bytes 4608 | tf_op jit(solution)/shard_map/all_gather | solution.py:129
  186.1 29.2 %all_gather.70 = bf16[512,512]{1,0:T(8,128)(2,1)S(1)} all-gather(bf16[64,512]{1,0:T(8,128)(2,1)S(1)} %copy-done.117), channel_id=1, replica_groups=mesh['ctx'=16,'wt'=8] {'wt'}, dimensions={0}, use_global_device_ids=true | all-gather | bytes 589824 | tf_op jit(solution)/shard_map/all_gather | solution.py:155
  222.0 29.3 %all_gather.72 = bf16[512,512]{1,0:T(8,128)(2,1)S(1)} all-gather(bf16[64,512]{1,0:T(8,128)(2,1)S(1)} %copy-done.118), channel_id=1, replica_groups=mesh['ctx'=16,'wt'=8] {'wt'}, dimensions={0}, use_global_device_ids=true | all-gather | bytes 589824 | tf_op jit(solution)/shard_map/all_gather | solution.py:156
  253.5 29.9 %all_gather.69 = bf16[512,512]{1,0:T(8,128)(2,1)S(1)} all-gather(bf16[64,512]{1,0:T(8,128)(2,1)S(1)} %copy-done.119), channel_id=1, replica_groups=mesh['ctx'=16,'wt'=8] {'wt'}, dimensions={0}, use_global_device_ids=true | all-gather | bytes 589824 | tf_op jit(solution)/shard_map/all_gather | solution.py:154
  283.4 29.6 %all_gather.74 = bf16[512,512]{1,0:T(8,128)(2,1)S(1)} all-gather(bf16[64,512]{1,0:T(8,128)(2,1)S(1)} %copy-done.120), channel_id=1, replica_groups=mesh['ctx'=16,'wt'=8] {'wt'}, dimensions={0}, use_global_device_ids=true | all-gather | bytes 589824 | tf_op jit(solution)/shard_map/all_gather | solution.py:157
  369.1 14.9 %all-gather.16.cloned.1.call-done = bf16[512,2048]{1,0:T(8,128)(2,1)} async-done(((bf16[64,2048]{1,0:T(8,128)(2,1)}), bf16[512,2048]{1,0:T(8,128)(2,1)}) %all-gather.16.cloned.1.call-update) | async-done | bytes 2097168 | tf_op jit(solution)/shard_map/all_gather | solution.py:183
  387.8 38.5 %all-gather.18.cloned.1.call-done = bf16[2048,512]{1,0:T(8,128)(2,1)} async-done(((bf16[256,512]{1,0:T(8,128)(2,1)}), bf16[2048,512]{1,0:T(8,128)(2,1)}) %all-gather.18.cloned.1.call-update) | async-done | bytes 2097168 | tf_op jit(solution)/shard_map/all_gather | solution.py:184
  470.7 4.0 fusion.31
  522.4 27.9 %reduce-scatter.15.cloned.1.call-done = bf16[256,512]{0,1:T(8,128)(2,1)} async-done(((bf16[4096,512]{0,1:T(8,128)(2,1)}), bf16[256,512]{0,1:T(8,128)(2,1)}) %reduce-scatter.15.cloned.1.call-update) | async-done | bytes 262160 | tf_op jit(solution)/shard_map/reduce_scatter | solution.py:233
  551.8 82.4 %reduce-scatter.17.cloned.1.call-done = bf16[256,512]{0,1:T(8,128)(2,1)} async-done(((bf16[4096,512]{0,1:T(8,128)(2,1)}), bf16[256,512]{0,1:T(8,128)(2,1)}) %reduce-scatter.17.cloned.1.call-update) | async-done | bytes 262160 | tf_op jit(solution)/shard_map/reduce_scatter | solution.py:239
  638.2 11.4 fusion.80
  656.3 12.4 multiply_reduce_fusion.8
  671.8 3.9 collective-permute-start.7
  692.4 20.0 %reduce-scatter.31.cloned.1.call-done = bf16[64,512]{1,0:T(8,128)(2,1)} async-done(((bf16[512,512]{1,0:T(8,128)(2,1)}), bf16[64,512]{1,0:T(8,128)(2,1)}) %reduce-scatter.31.cloned.1.call-update) | async-done | bytes 65552 | tf_op jit(solution)/shard_map/reduce_scatter | solution.py:259
  712.4 44.0 %reduce-scatter.41.cloned.1.call-done = bf16[256,512]{1,0:T(8,128)(2,1)} async-done(((bf16[2048,512]{1,0:T(8,128)(2,1)}), bf16[256,512]{1,0:T(8,128)(2,1)}) %reduce-scatter.41.cloned.1.call-update) | async-done | bytes 262160 | tf_op jit(solution)/shard_map/reduce_scatter | solution.py:205
  756.4 43.6 %reduce-scatter.39.cloned.1.call-done = bf16[64,2048]{1,0:T(8,128)(2,1)} async-done(((bf16[512,2048]{1,0:T(8,128)(2,1)}), bf16[64,2048]{1,0:T(8,128)(2,1)}) %reduce-scatter.39.cloned.1.call-update) | async-done | bytes 262160 | tf_op jit(solution)/shard_map/reduce_scatter | solution.py:202
  800.0 38.9 %reduce-scatter.35.cloned.1.call-done = bf16[64,512]{1,0:T(8,128)(2,1)} async-done(((bf16[512,512]{1,0:T(8,128)(2,1)}), bf16[64,512]{1,0:T(8,128)(2,1)}) %reduce-scatter.35.cloned.1.call-update) | async-done | bytes 65552 | tf_op jit(solution)/shard_map/reduce_scatter | solution.py:265
  838.9 39.6 %reduce-scatter.33.cloned.1.call-done = bf16[64,512]{1,0:T(8,128)(2,1)} async-done(((bf16[512,512]{1,0:T(8,128)(2,1)}), bf16[64,512]{1,0:T(8,128)(2,1)}) %reduce-scatter.33.cloned.1.call-update) | async-done | bytes 65552 | tf_op jit(solution)/shard_map/reduce_scatter | solution.py:262
  878.5 39.5 %reduce-scatter.21.cloned.1.call-done = bf16[64,512]{1,0:T(8,128)(2,1)} async-done(((bf16[512,512]{1,0:T(8,128)(2,1)}), bf16[64,512]{1,0:T(8,128)(2,1)}) %reduce-scatter.21.cloned.1.call-update) | async-done | bytes 65552 | tf_op jit(solution)/shard_map/reduce_scatter | solution.py:337
  918.0 39.6 %reduce-scatter.19.cloned.1.call-done = bf16[64,512]{1,0:T(8,128)(2,1)} async-done(((bf16[512,512]{1,0:T(8,128)(2,1)}), bf16[64,512]{1,0:T(8,128)(2,1)}) %reduce-scatter.19.cloned.1.call-update) | async-done | bytes 65552 | tf_op jit(solution)/shard_map/reduce_scatter | solution.py:334
  957.6 39.6 %reduce-scatter.25.cloned.1.call-done = bf16[3,64,256]{2,1,0:T(8,128)(2,1)} async-done(((bf16[3,512,256]{2,1,0:T(8,128)(2,1)}), bf16[3,64,256]{2,1,0:T(8,128)(2,1)}) %reduce-scatter.25.cloned.1.call-update) | async-done | bytes 98320 | tf_op jit(solution)/shard_map/reduce_scatter | solution.py:310
  997.2 40.3 %reduce-scatter.29.cloned.1.call-done = bf16[256,256]{1,0:T(8,128)(2,1)} async-done(((bf16[2048,256]{1,0:T(8,128)(2,1)}), bf16[256,256]{1,0:T(8,128)(2,1)}) %reduce-scatter.29.cloned.1.call-update) | async-done | bytes 131088 | tf_op jit(solution)/shard_map/reduce_scatter | solution.py:319
  1037.4 44.0 %reduce-scatter.23.cloned.1.call-done = bf16[64,2048]{1,0:T(8,128)(2,1)} async-done(((bf16[512,2048]{1,0:T(8,128)(2,1)}), bf16[64,2048]{1,0:T(8,128)(2,1)}) %reduce-scatter.23.cloned.1.call-update) | async-done | bytes 262160 | tf_op jit(solution)/shard_map/reduce_scatter | solution.py:307
  1086.2 16.6 %all-reduce.13 = (bf16[512]{0:T(512)(128)(2,1)S(1)}, bf16[512]{0:T(512)(128)(2,1)S(1)}, bf16[2048]{0:T(1024)(128)(2,1)S(1)}, bf16[512]{0:T(512)(128)(2,1)S(1)}, bf16[512]{0:T(512)(128)(2,1)S(1)}) all-reduce(bf16[512]{0:T(512)(128)(2,1)S(1)} %get-tuple-element.41, ...), channel_id=4, replica_groups=mesh['ctx'=16,'wt'=8] {'wt'}, use_global_device_ids=true, to_apply=%region_47.48.clone | all-reduce | flops 4096 | bytes 16384
  1104.3 15.9 %reduce-scatter.27.cloned.1.call-done = bf16[9,256]{1,0:T(8,128)(2,1)} async-done(((bf16[9,2048]{1,0:T(8,128)(2,1)}), bf16[9,256]{1,0:T(8,128)(2,1)}) %reduce-scatter.27.cloned.1.call-update) | async-done | bytes 4624 | tf_op jit(solution)/shard_map/reduce_scatter | solution.py:316
  1120.2 65.0 %all-reduce.11 = (bf16[64]{0:T(256)(128)(2,1)S(1)}, bf16[64]{0:T(256)(128)(2,1)S(1)}, bf16[256]{0:T(256)(128)(2,1)S(1)}, bf16[9,256]{1,0:T(8,128)(2,1)S(1)}, bf1...) all-reduce(bf16[64]{0:T(256)(128)(2,1)S(1)} %dynamic-slice.5, ...), channel_id=1, replica_groups=mesh['ctx'=16,'wt'=8] {'ctx'}, use_global_device_ids=true, to_apply=%region_48.49 | all-reduce | flops 2816 | bytes 11264 | tf_op jit(solution)/shard_map/psum | solution.py:342
  1188.4 78.5 %all-reduce.17.cloned.1.call-done = (bf16[64,512]{1,0:T(8,128)(2,1)}, bf16[64,512]{1,0:T(8,128)(2,1)}, bf16[64,2048]{1,0:T(8,128)(2,1)}, bf16[3,64,256]{2,1,0:T(...) async-done(((bf16[64,512]{1,0:T(8,128)(2,1)}, ...) | async-done | bytes 1409040 | tf_op jit(solution)/shard_map/psum | solution.py:343
  (575 shorter events, 237.7 us)
Async XLA Ops:
  7.2 171.1 %all-gather.8.cloned.1.call-start = ((), (), s32[]{:S(2)}) async-start(), calls=%async_computation.14 | async-start | bytes 2359296 | tf_op jit(solution)/shard_map/all_gather | solution.py:127
  7.9 210.4 %all-gather.10.cloned.1.call-start = ((), (), s32[]{:S(2)}) async-start(), calls=%async_computation.15 | async-start | bytes 1179648 | tf_op jit(solution)/shard_map/all_gather | solution.py:131
  99.7 120.7 %copy-start.47 = (f32[256,512]{1,0:T(8,128)}, f32[256,512]{1,0:T(8,128)S(1)}, u32[]{:S(2)}) copy-start(f32[256,512]{1,0:T(8,128)S(1)} %get-tuple-element.83) | copy-start | bytes 1572868
  100.1 77.1 %collective-permute-start = (bf16[1,512]{1,0:T(2,128)(2,1)S(1)}, bf16[1,512]{1,0:T(2,128)(2,1)S(1)}, u32[]{:S(2)}, u32[]{:S(2)}) collective-permute-start(bf16[1,512]{1,0:T(2,128)(2,1)S(1)} %get-tuple-element.88), channel_id=1, source_target_pairs={{0,8},{8,16},{16,24},{24,32},{32,40},{40,48},{48,56},{56,64},{64,7... | collective-permute-start | bytes 3080 | tf_op jit(solution)/shard_map/ppermute | solution.py:16
  101.4 75.8 %collective-permute-start.1 = (bf16[1,512]{1,0:T(2,128)(2,1)S(1)}, bf16[1,512]{1,0:T(2,128)(2,1)S(1)}, u32[]{:S(2)}, u32[]{:S(2)}) collective-permute-start(bf16[1,512]{1,0:T(2,128)(2,1)S(1)} %get-tuple-element.89), channel_id=1, source_target_pairs={{8,0},{16,8},{24,16},{32,24},{40,32},{48,40},{56,48},{64,56},{72,6... | collective-permute-start | bytes 3080 | tf_op jit(solution)/shard_map/ppermute | solution.py:19
  102.7 211.3 %all-gather.12.cloned.1.call-start = ((), (), s32[]{:S(2)}) async-start(), calls=%async_computation.16 | async-start | bytes 4456448 | tf_op jit(solution)/shard_map/all_gather | solution.py:165
  183.5 31.9 %collective-permute-start.2 = (bf16[4,2048]{1,0:T(4,128)(2,1)S(1)}, bf16[4,2048]{1,0:T(4,128)(2,1)S(1)}, u32[]{:S(2)}, u32[]{:S(2)}) collective-permute-start(bf16[4,2048]{1,0:T(4,128)(2,1)S(1)} %get-tuple-element.86), channel_id=1, source_target_pairs={{0,8},{8,16},{16,24},{24,32},{32,40},{40,48},{48,56},{56,64},{64,7... | collective-permute-start | bytes 49160 | tf_op jit(solution)/shard_map/ppermute | solution.py:16
  184.8 30.6 %collective-permute-start.3 = (bf16[4,2048]{1,0:T(4,128)(2,1)S(1)}, bf16[4,2048]{1,0:T(4,128)(2,1)S(1)}, u32[]{:S(2)}, u32[]{:S(2)}) collective-permute-start(bf16[4,2048]{1,0:T(4,128)(2,1)S(1)} %get-tuple-element.87), channel_id=1, source_target_pairs={{8,0},{16,8},{24,16},{32,24},{40,32},{48,40},{56,48},{64,56},{72,6... | collective-permute-start | bytes 49160 | tf_op jit(solution)/shard_map/ppermute | solution.py:19
  221.9 126.5 %all-gather.14.cloned.1.call-start = ((), (), s32[]{:S(2)}) async-start(), calls=%async_computation.17 | async-start | bytes 4456448 | tf_op jit(solution)/shard_map/all_gather | solution.py:166
  252.3 131.8 %all-gather.16.cloned.1.call-start = ((), (), s32[]{:S(2)}) async-start(), calls=%async_computation.18 | async-start | bytes 2359296 | tf_op jit(solution)/shard_map/all_gather | solution.py:183
  252.9 173.4 %all-gather.18.cloned.1.call-start = ((), (), s32[]{:S(2)}) async-start(), calls=%async_computation.19 | async-start | bytes 2359296 | tf_op jit(solution)/shard_map/all_gather | solution.py:184
  253.4 296.8 %reduce-scatter.15.cloned.1.call-start = ((), (), s32[]{:S(2)}) async-start(), calls=%async_computation.20 | async-start | bytes 4456448 | tf_op jit(solution)/shard_map/reduce_scatter | solution.py:233
  470.7 163.5 %reduce-scatter.17.cloned.1.call-start = ((), (), s32[]{:S(2)}) async-start(), calls=%async_computation.21 | async-start | bytes 4456448 | tf_op jit(solution)/shard_map/reduce_scatter | solution.py:239
  491.8 200.6 %reduce-scatter.37.cloned.1.call-start = ((), (), s32[]{:S(2)}) async-start(), calls=%async_computation.31 | async-start | bytes 589824 | tf_op jit(solution)/shard_map/reduce_scatter | solution.py:268
  494.1 218.3 %reduce-scatter.31.cloned.1.call-start = ((), (), s32[]{:S(2)}) async-start(), calls=%async_computation.28 | async-start | bytes 589824 | tf_op jit(solution)/shard_map/reduce_scatter | solution.py:259
  511.3 245.0 %reduce-scatter.41.cloned.1.call-start = ((), (), s32[]{:S(2)}) async-start(), calls=%async_computation.33 | async-start | bytes 2359296 | tf_op jit(solution)/shard_map/reduce_scatter | solution.py:205
  515.2 284.8 %reduce-scatter.39.cloned.1.call-start = ((), (), s32[]{:S(2)}) async-start(), calls=%async_computation.32 | async-start | bytes 2359296 | tf_op jit(solution)/shard_map/reduce_scatter | solution.py:202
  518.7 320.3 %reduce-scatter.35.cloned.1.call-start = ((), (), s32[]{:S(2)}) async-start(), calls=%async_computation.30 | async-start | bytes 589824 | tf_op jit(solution)/shard_map/reduce_scatter | solution.py:265
  518.7 115.4 %copy-start.61 = (bf16[512,512]{1,0:T(8,128)(2,1)S(1)}, bf16[512,512]{1,0:T(8,128)(2,1)}, u32[]{:S(2)}) copy-start(bf16[512,512]{1,0:T(8,128)(2,1)} %copy-done.60) | copy-start | bytes 1572868
  551.8 86.0 %copy-start.52 = (f32[256,512]{1,0:T(8,128)S(1)}, f32[256,512]{1,0:T(8,128)}, u32[]{:S(2)}) copy-start(f32[256,512]{1,0:T(8,128)} %copy-done.51) | copy-start | bytes 1572868
  637.5 241.0 %reduce-scatter.33.cloned.1.call-start = ((), (), s32[]{:S(2)}) async-start(), calls=%async_computation.29 | async-start | bytes 589824 | tf_op jit(solution)/shard_map/reduce_scatter | solution.py:262
  650.5 5.6 collective-permute-start.4
  651.8 4.3 collective-permute-start.5
  656.1 262.0 %reduce-scatter.21.cloned.1.call-start = ((), (), s32[]{:S(2)}) async-start(), calls=%async_computation.23 | async-start | bytes 589824 | tf_op jit(solution)/shard_map/reduce_scatter | solution.py:337
  670.3 6.2 collective-permute-start.6
  671.8 4.8 collective-permute-start.7
  679.9 277.7 %reduce-scatter.19.cloned.1.call-start = ((), (), s32[]{:S(2)}) async-start(), calls=%async_computation.22 | async-start | bytes 589824 | tf_op jit(solution)/shard_map/reduce_scatter | solution.py:334
  681.4 315.8 %reduce-scatter.25.cloned.1.call-start = ((), (), s32[]{:S(2)}) async-start(), calls=%async_computation.25 | async-start | bytes 884736 | tf_op jit(solution)/shard_map/reduce_scatter | solution.py:310
  683.5 353.9 %reduce-scatter.29.cloned.1.call-start = ((), (), s32[]{:S(2)}) async-start(), calls=%async_computation.27 | async-start | bytes 1179648 | tf_op jit(solution)/shard_map/reduce_scatter | solution.py:319
  685.1 396.3 %reduce-scatter.23.cloned.1.call-start = ((), (), s32[]{:S(2)}) async-start(), calls=%async_computation.24 | async-start | bytes 2359296 | tf_op jit(solution)/shard_map/reduce_scatter | solution.py:307
  688.8 431.3 %reduce-scatter.27.cloned.1.call-start = ((), (), s32[]{:S(2)}) async-start(), calls=%async_computation.26 | async-start | bytes 73728 | tf_op jit(solution)/shard_map/reduce_scatter | solution.py:316
  691.0 575.9 %all-reduce.17.cloned.1.call-start = ((), (), s32[]{:S(2)}) async-start(), calls=%async_computation.34 | async-start | bytes 2818048 | tf_op jit(solution)/shard_map/psum | solution.py:343
  (156 other events, 2237.1 us)
Sparse Core Ops, SparseCore 0:
  9.7 45.4 all-gather.7
  102.9 42.5 all-gather.9
  222.0 65.0 all-gather.11
  290.0 52.5 all-gather.13
  344.1 39.8 all-gather.15
  385.5 40.7 all-gather.17
  470.8 79.4 reduce-scatter.14
  554.8 79.2 reduce-scatter.16
  636.5 36.8 reduce-scatter.36
  675.7 36.6 reduce-scatter.30
  714.8 41.5 reduce-scatter.40
  758.6 41.3 reduce-scatter.38
  802.4 36.5 reduce-scatter.34
  841.9 36.6 reduce-scatter.32
  881.3 36.6 reduce-scatter.20
  920.9 36.6 reduce-scatter.18
  959.8 37.2 reduce-scatter.24
  999.5 37.8 reduce-scatter.28
  1040.0 41.4 reduce-scatter.22
  1084.3 35.7 reduce-scatter.26
  1123.6 143.2 all-reduce.16
where the time goes:
time: 1300 us; the launch traced here: 1290 us
  waiting for transfers between devices  649 us (50%)
  blocking collectives  354 us (27%)
  matrix products  146 us (11%)
  other arithmetic  58.8 us (5%)
  local copies, waits for them, and re-layouts  46 us (4%)
  between operations  19.5 us (2%)
  starting transfers between devices  16.5 us (1%)
    reduce_scatter x1, waiting for transfers between devices, shards(): lax.psum_scatter(jnp.concatenate(value_grads, 1).astype(jnp.bfloat16), 'c...  82.4 us
    psum x1, waiting for transfers between devices, shards(): lax.psum(s_wval.astype(jnp.bfloat16), 'ctx').astype(jnp.float32)  78.5 us
    psum x1, blocking collectives, shards(): lax.psum(s_gglu.astype(jnp.bfloat16), 'ctx').astype(jnp.float32)  65 us
    dot_general x27, matrix products, outer_cols(): lax.dot_general(left, right, (((1,), (1,)), ((), ())), preferred_element_...  52.7 us
    dot_general x27, matrix products, inner_rows(): lax.dot_general(left, right, (((0,), (0,)), ((), ())), preferred_element_...  47.8 us
    dot_general x27, matrix products, matmul(): return jnp.dot(left, right, preferred_element_type=jnp.float32)  45.4 us
    reduce_scatter x1, waiting for transfers between devices, shards(): lax.psum_scatter(d_wid.astype(jnp.bfloat16), 'wt', scatter_dimension=0, t...  44 us
    reduce_scatter x1, waiting for transfers between devices, shards(): lax.psum_scatter(d_lower.astype(jnp.bfloat16), 'wt', scatter_dimension=0,...  44 us
  transfers between devices with their start and end apart: 29, of which 16 were waited for; matrix products, arithmetic and copies ran while one was open for 12% of the time, Pallas kernels for 0%

commit v1 on v0

--- a/solution.py
+++ b/solution.py
@@ -340,7 +340,7 @@
     )
     summed = (
         lax.psum(s_gglu.astype(jnp.bfloat16), "ctx").astype(jnp.float32),
-        lax.psum(s_wval.astype(jnp.bfloat16), "ctx").astype(jnp.float32),
+        jnp.sum(lax.all_gather(s_wval.astype(jnp.bfloat16), "ctx"), axis=0).astype(jnp.float32),
         lax.psum(s_wgat.astype(jnp.bfloat16), "ctx").astype(jnp.float32),
         lax.psum(s_gconv.astype(jnp.bfloat16), "ctx").astype(jnp.float32),
         lax.psum(s_wid.astype(jnp.bfloat16), "ctx").astype(jnp.float32),

time: 1300 us -> 1390 us (1.069)
  waiting for transfers between devices: 649 us -> 745 us
    psum x1, waiting for transfers between devices: 78.5 us -> 121 us  [shards(): lax.psum(s_wgat.astype(jnp.bfloat16), 'ctx').astype(jnp.float32)]
    reduce_scatter x1, waiting for transfers between devices: 0.02 us -> 37.7 us  [shards(): lax.psum_scatter(d_outp.astype(jnp.bfloat16), 'wt', scatter_dimension=0,...]
    reduce_scatter x1, waiting for transfers between devices: 20 us -> 39.1 us  [shards(): lax.psum_scatter(d_qry.astype(jnp.bfloat16), 'wt', scatter_dimension=0, t...]
    reduce_scatter x1, waiting for transfers between devices: 39.6 us -> 20.6 us  [shards(): lax.psum_scatter(d_wval.astype(jnp.bfloat16), 'wt', scatter_dimension=0,...]
    reduce_scatter x1, waiting for transfers between devices: 27.9 us -> 42.9 us  [shards(): lax.psum_scatter(jnp.concatenate(key_grads, 1).astype(jnp.bfloat16), 'ctx...]
    unnamed x333 -> x341, local copies, waits for them, and re-layouts: 42 us -> 40.3 us
  transfers between devices with their start and end apart: 29 -> 30, of which waited for: 16 -> 17; matrix products, arithmetic and copies ran while one was open for 12% -> 9% of each run, Pallas kernels for 0% -> 0%
where the time goes in v1:
time: 1390 us; the launch traced here: 1380 us
  waiting for transfers between devices  745 us (54%)
  blocking collectives  353 us (25%)
  matrix products  138 us (10%)
  other arithmetic  62 us (4%)
  local copies, waits for them, and re-layouts  44.7 us (3%)
  between operations  19.5 us (1%)
  starting transfers between devices  16.6 us (1%)
    psum x1, waiting for transfers between devices, shards(): lax.psum(s_wgat.astype(jnp.bfloat16), 'ctx').astype(jnp.float32)  121 us
    reduce_scatter x1, waiting for transfers between devices, shards(): lax.psum_scatter(jnp.concatenate(value_grads, 1).astype(jnp.bfloat16), 'c...  82.4 us
    psum x1, blocking collectives, shards(): lax.psum(s_gglu.astype(jnp.bfloat16), 'ctx').astype(jnp.float32)  65 us
    dot_general x27, matrix products, inner_rows(): lax.dot_general(left, right, (((0,), (0,)), ((), ())), preferred_element_...  47 us
    dot_general x27, matrix products, outer_cols(): lax.dot_general(left, right, (((1,), (1,)), ((), ())), preferred_element_...  45.7 us
    dot_general x27, matrix products, matmul(): return jnp.dot(left, right, preferred_element_type=jnp.float32)  45.6 us
    reduce_scatter x1, waiting for transfers between devices, shards(): lax.psum_scatter(d_upper.astype(jnp.bfloat16), 'wt', scatter_dimension=0,...  44.2 us
    reduce_scatter x1, waiting for transfers between devices, shards(): lax.psum_scatter(d_wid.astype(jnp.bfloat16), 'wt', scatter_dimension=0, t...  44.1 us
  transfers between devices with their start and end apart: 30, of which 17 were waited for; matrix products, arithmetic and copies ran while one was open for 9% of the time, Pallas kernels for 0%

profile of v1, /device:TPU:0, one launch (start us, length us, event | category | flops | bytes accessed | tf_op | source)
XLA Modules:
  0.0 1378.2 jit_solution(5928759353621898256)
XLA Ops:
  14.0 21.1 %all-reduce.14 = (bf16[512]{0:T(512)(128)(2,1)S(1)}, bf16[512]{0:T(512)(128)(2,1)S(1)}, bf16[512]{0:T(512)(128)(2,1)S(1)}, bf16[512]{0:T(512)(128)(2,1)S(1)}) all-reduce(bf16[512]{0:T(512)(128)(2,1)S(1)} %dynamic-update-slice, bf16[512]{0:T(512)(128)(2,1)S(1)} %dynamic-update-slice.1, ...), channel_id=1, replica_groups=mesh['ctx'=16,'wt'=8] {'wt'}, use_global_device_ids=true, to_apply=%add.2 | all-reduce | flops 2048 | bytes 8192
  38.0 29.6 %all_gather.66 = bf16[512,512]{1,0:T(8,128)(2,1)S(1)} all-gather(bf16[64,512]{1,0:T(8,128)(2,1)} %param.24), channel_id=1, replica_groups=mesh['ctx'=16,'wt'=8] {'wt'}, dimensions={0}, use_global_device_ids=true | all-gather | bytes 589824 | tf_op jit(solution)/shard_map/all_gather | solution.py:116
  67.5 29.2 %all_gather.67 = bf16[512,512]{1,0:T(8,128)(2,1)S(1)} all-gather(bf16[64,512]{1,0:T(8,128)(2,1)} %param.25), channel_id=1, replica_groups=mesh['ctx'=16,'wt'=8] {'wt'}, dimensions={0}, use_global_device_ids=true | all-gather | bytes 589824 | tf_op jit(solution)/shard_map/all_gather | solution.py:117
  104.0 28.2 %all_gather.72 = bf16[9,2048]{1,0:T(8,128)(2,1)S(1)} all-gather(bf16[9,256]{1,0:T(8,128)(2,1)S(1)} %copy-done.144), channel_id=1, replica_groups=mesh['ctx'=16,'wt'=8] {'wt'}, dimensions={1}, use_global_device_ids=true | all-gather | bytes 41472 | tf_op jit(solution)/shard_map/all_gather | solution.py:130
  132.4 29.8 %all_gather.70 = bf16[3,512,256]{2,1,0:T(8,128)(2,1)S(1)} all-gather(bf16[3,64,256]{2,1,0:T(8,128)(2,1)S(1)} %copy-done.102), channel_id=1, replica_groups=mesh['ctx'=16,'wt'=8] {'wt'}, dimensions={1}, use_global_device_ids=true | all-gather | bytes 884736 | tf_op jit(solution)/shard_map/all_gather | solution.py:128
  162.2 16.1 %all-gather.1 = bf16[8,1,256]{2,1,0:T(2,128)(2,1)S(1)} all-gather(bf16[1,1,256]{2,1,0:T(2,128)(2,1)S(1)} %reshape.268), channel_id=1, replica_groups=mesh['ctx'=16,'wt'=8] {'wt'}, dimensions={0}, use_global_device_ids=true | all-gather | bytes 4608 | tf_op jit(solution)/shard_map/all_gather | solution.py:129
  187.6 29.1 %all_gather.76 = bf16[512,512]{1,0:T(8,128)(2,1)S(1)} all-gather(bf16[64,512]{1,0:T(8,128)(2,1)S(1)} %copy-done.121), channel_id=1, replica_groups=mesh['ctx'=16,'wt'=8] {'wt'}, dimensions={0}, use_global_device_ids=true | all-gather | bytes 589824 | tf_op jit(solution)/shard_map/all_gather | solution.py:155
  223.4 29.0 %all_gather.78 = bf16[512,512]{1,0:T(8,128)(2,1)S(1)} all-gather(bf16[64,512]{1,0:T(8,128)(2,1)S(1)} %copy-done.122), channel_id=1, replica_groups=mesh['ctx'=16,'wt'=8] {'wt'}, dimensions={0}, use_global_device_ids=true | all-gather | bytes 589824 | tf_op jit(solution)/shard_map/all_gather | solution.py:156
  255.4 29.8 %all_gather.75 = bf16[512,512]{1,0:T(8,128)(2,1)S(1)} all-gather(bf16[64,512]{1,0:T(8,128)(2,1)S(1)} %copy-done.123), channel_id=1, replica_groups=mesh['ctx'=16,'wt'=8] {'wt'}, dimensions={0}, use_global_device_ids=true | all-gather | bytes 589824 | tf_op jit(solution)/shard_map/all_gather | solution.py:154
  285.3 29.3 %all_gather.80 = bf16[512,512]{1,0:T(8,128)(2,1)S(1)} all-gather(bf16[64,512]{1,0:T(8,128)(2,1)S(1)} %copy-done.124), channel_id=1, replica_groups=mesh['ctx'=16,'wt'=8] {'wt'}, dimensions={0}, use_global_device_ids=true | all-gather | bytes 589824 | tf_op jit(solution)/shard_map/all_gather | solution.py:157
  370.8 14.9 %all-gather.18.cloned.1.call-done = bf16[512,2048]{1,0:T(8,128)(2,1)} async-done(((bf16[64,2048]{1,0:T(8,128)(2,1)}), bf16[512,2048]{1,0:T(8,128)(2,1)}) %all-gather.18.cloned.1.call-update) | async-done | bytes 2097168 | tf_op jit(solution)/shard_map/all_gather | solution.py:183
  389.4 38.6 %all-gather.20.cloned.1.call-done = bf16[2048,512]{1,0:T(8,128)(2,1)} async-done(((bf16[256,512]{1,0:T(8,128)(2,1)}), bf16[2048,512]{1,0:T(8,128)(2,1)}) %all-gather.20.cloned.1.call-update) | async-done | bytes 2097168 | tf_op jit(solution)/shard_map/all_gather | solution.py:184
  472.8 4.0 fusion.31
  509.4 42.9 %reduce-scatter.15.cloned.1.call-done = bf16[256,512]{0,1:T(8,128)(2,1)} async-done(((bf16[4096,512]{0,1:T(8,128)(2,1)}), bf16[256,512]{0,1:T(8,128)(2,1)}) %reduce-scatter.15.cloned.1.call-update) | async-done | bytes 262160 | tf_op jit(solution)/shard_map/reduce_scatter | solution.py:233
  553.8 82.4 %reduce-scatter.17.cloned.1.call-done = bf16[256,512]{0,1:T(8,128)(2,1)} async-done(((bf16[4096,512]{0,1:T(8,128)(2,1)}), bf16[256,512]{0,1:T(8,128)(2,1)}) %reduce-scatter.17.cloned.1.call-update) | async-done | bytes 262160 | tf_op jit(solution)/shard_map/reduce_scatter | solution.py:239
  638.8 4.2 fusion.80
  651.8 12.3 multiply_reduce_fusion.8
  698.9 20.6 %reduce-scatter.19.cloned.1.call-done = bf16[64,512]{1,0:T(8,128)(2,1)} async-done(((bf16[512,512]{1,0:T(8,128)(2,1)}), bf16[64,512]{1,0:T(8,128)(2,1)}) %reduce-scatter.19.cloned.1.call-update) | async-done | bytes 65552 | tf_op jit(solution)/shard_map/reduce_scatter | solution.py:334
  720.9 37.7 %reduce-scatter.37.cloned.1.call-done = bf16[64,512]{1,0:T(8,128)(2,1)} async-done(((bf16[512,512]{1,0:T(8,128)(2,1)}), bf16[64,512]{1,0:T(8,128)(2,1)}) %reduce-scatter.37.cloned.1.call-update) | async-done | bytes 65552 | tf_op jit(solution)/shard_map/reduce_scatter | solution.py:268
  758.5 39.1 %reduce-scatter.31.cloned.1.call-done = bf16[64,512]{1,0:T(8,128)(2,1)} async-done(((bf16[512,512]{1,0:T(8,128)(2,1)}), bf16[64,512]{1,0:T(8,128)(2,1)}) %reduce-scatter.31.cloned.1.call-update) | async-done | bytes 65552 | tf_op jit(solution)/shard_map/reduce_scatter | solution.py:259
  797.6 43.9 %reduce-scatter.41.cloned.1.call-done = bf16[256,512]{1,0:T(8,128)(2,1)} async-done(((bf16[2048,512]{1,0:T(8,128)(2,1)}), bf16[256,512]{1,0:T(8,128)(2,1)}) %reduce-scatter.41.cloned.1.call-update) | async-done | bytes 262160 | tf_op jit(solution)/shard_map/reduce_scatter | solution.py:205
  841.5 44.2 %reduce-scatter.39.cloned.1.call-done = bf16[64,2048]{1,0:T(8,128)(2,1)} async-done(((bf16[512,2048]{1,0:T(8,128)(2,1)}), bf16[64,2048]{1,0:T(8,128)(2,1)}) %reduce-scatter.39.cloned.1.call-update) | async-done | bytes 262160 | tf_op jit(solution)/shard_map/reduce_scatter | solution.py:202
  885.7 38.6 %reduce-scatter.35.cloned.1.call-done = bf16[64,512]{1,0:T(8,128)(2,1)} async-done(((bf16[512,512]{1,0:T(8,128)(2,1)}), bf16[64,512]{1,0:T(8,128)(2,1)}) %reduce-scatter.35.cloned.1.call-update) | async-done | bytes 65552 | tf_op jit(solution)/shard_map/reduce_scatter | solution.py:265
  924.3 38.9 %reduce-scatter.33.cloned.1.call-done = bf16[64,512]{1,0:T(8,128)(2,1)} async-done(((bf16[512,512]{1,0:T(8,128)(2,1)}), bf16[64,512]{1,0:T(8,128)(2,1)}) %reduce-scatter.33.cloned.1.call-update) | async-done | bytes 65552 | tf_op jit(solution)/shard_map/reduce_scatter | solution.py:262
  963.2 39.6 %reduce-scatter.21.cloned.1.call-done = bf16[64,512]{1,0:T(8,128)(2,1)} async-done(((bf16[512,512]{1,0:T(8,128)(2,1)}), bf16[64,512]{1,0:T(8,128)(2,1)}) %reduce-scatter.21.cloned.1.call-update) | async-done | bytes 65552 | tf_op jit(solution)/shard_map/reduce_scatter | solution.py:337
  1002.8 39.5 %reduce-scatter.25.cloned.1.call-done = bf16[3,64,256]{2,1,0:T(8,128)(2,1)} async-done(((bf16[3,512,256]{2,1,0:T(8,128)(2,1)}), bf16[3,64,256]{2,1,0:T(8,128)(2,1)}) %reduce-scatter.25.cloned.1.call-update) | async-done | bytes 98320 | tf_op jit(solution)/shard_map/reduce_scatter | solution.py:310
  1042.3 40.3 %reduce-scatter.29.cloned.1.call-done = bf16[256,256]{1,0:T(8,128)(2,1)} async-done(((bf16[2048,256]{1,0:T(8,128)(2,1)}), bf16[256,256]{1,0:T(8,128)(2,1)}) %reduce-scatter.29.cloned.1.call-update) | async-done | bytes 131088 | tf_op jit(solution)/shard_map/reduce_scatter | solution.py:319
  1082.7 44.1 %reduce-scatter.23.cloned.1.call-done = bf16[64,2048]{1,0:T(8,128)(2,1)} async-done(((bf16[512,2048]{1,0:T(8,128)(2,1)}), bf16[64,2048]{1,0:T(8,128)(2,1)}) %reduce-scatter.23.cloned.1.call-update) | async-done | bytes 262160 | tf_op jit(solution)/shard_map/reduce_scatter | solution.py:307
  1131.6 16.6 %all-reduce.13 = (bf16[512]{0:T(512)(128)(2,1)S(1)}, bf16[512]{0:T(512)(128)(2,1)S(1)}, bf16[2048]{0:T(1024)(128)(2,1)S(1)}, bf16[512]{0:T(512)(128)(2,1)S(1)}, bf16[512]{0:T(512)(128)(2,1)S(1)}) all-reduce(bf16[512]{0:T(512)(128)(2,1)S(1)} %get-tuple-element.41, ...), channel_id=5, replica_groups=mesh['ctx'=16,'wt'=8] {'wt'}, use_global_device_ids=true, to_apply=%region_47.48.clone | all-reduce | flops 4096 | bytes 16384
  1149.6 15.6 %reduce-scatter.27.cloned.1.call-done = bf16[9,256]{1,0:T(8,128)(2,1)} async-done(((bf16[9,2048]{1,0:T(8,128)(2,1)}), bf16[9,256]{1,0:T(8,128)(2,1)}) %reduce-scatter.27.cloned.1.call-update) | async-done | bytes 4624 | tf_op jit(solution)/shard_map/reduce_scatter | solution.py:316
  1165.2 65.0 %all-reduce.11 = (bf16[64]{0:T(256)(128)(2,1)S(1)}, bf16[64]{0:T(256)(128)(2,1)S(1)}, bf16[256]{0:T(256)(128)(2,1)S(1)}, bf16[9,256]{1,0:T(8,128)(2,1)S(1)}, bf1...) all-reduce(bf16[64]{0:T(256)(128)(2,1)S(1)} %dynamic-slice.5, ...), channel_id=1, replica_groups=mesh['ctx'=16,'wt'=8] {'ctx'}, use_global_device_ids=true, to_apply=%region_48.49 | all-reduce | flops 2816 | bytes 11264 | tf_op jit(solution)/shard_map/psum | solution.py:342
  1235.5 121.4 %all-reduce.17.cloned.1.call-done = (bf16[64,512]{1,0:T(8,128)(2,1)}, bf16[64,2048]{1,0:T(8,128)(2,1)}, bf16[3,64,256]{2,1,0:T(8,128)(2,1)}, bf16[256,256]{1,0:T...) async-done(((bf16[64,512]{1,0:T(8,128)(2,1)}, ...) | async-done | bytes 1343504 | tf_op jit(solution)/shard_map/psum | solution.py:344
  (587 shorter events, 243.0 us)
Async XLA Ops:
  7.2 172.3 %all-gather.10.cloned.1.call-start = ((), (), s32[]{:S(2)}) async-start(), calls=%async_computation.14 | async-start | bytes 2359296 | tf_op jit(solution)/shard_map/all_gather | solution.py:127
  7.9 211.7 %all-gather.12.cloned.1.call-start = ((), (), s32[]{:S(2)}) async-start(), calls=%async_computation.15 | async-start | bytes 1179648 | tf_op jit(solution)/shard_map/all_gather | solution.py:131
  101.3 77.0 %collective-permute-start = (bf16[1,512]{1,0:T(2,128)(2,1)S(1)}, bf16[1,512]{1,0:T(2,128)(2,1)S(1)}, u32[]{:S(2)}, u32[]{:S(2)}) collective-permute-start(bf16[1,512]{1,0:T(2,128)(2,1)S(1)} %get-tuple-element.87), channel_id=1, source_target_pairs={{0,8},{8,16},{16,24},{24,32},{32,40},{40,48},{48,56},{56,64},{64,7... | collective-permute-start | bytes 3080 | tf_op jit(solution)/shard_map/ppermute | solution.py:16
  102.6 75.7 %collective-permute-start.1 = (bf16[1,512]{1,0:T(2,128)(2,1)S(1)}, bf16[1,512]{1,0:T(2,128)(2,1)S(1)}, u32[]{:S(2)}, u32[]{:S(2)}) collective-permute-start(bf16[1,512]{1,0:T(2,128)(2,1)S(1)} %get-tuple-element.88), channel_id=1, source_target_pairs={{8,0},{16,8},{24,16},{32,24},{40,32},{48,40},{56,48},{64,56},{72,6... | collective-permute-start | bytes 3080 | tf_op jit(solution)/shard_map/ppermute | solution.py:19
  103.9 211.7 %all-gather.14.cloned.1.call-start = ((), (), s32[]{:S(2)}) async-start(), calls=%async_computation.16 | async-start | bytes 4456448 | tf_op jit(solution)/shard_map/all_gather | solution.py:165
  185.0 31.7 %collective-permute-start.2 = (bf16[4,2048]{1,0:T(4,128)(2,1)S(1)}, bf16[4,2048]{1,0:T(4,128)(2,1)S(1)}, u32[]{:S(2)}, u32[]{:S(2)}) collective-permute-start(bf16[4,2048]{1,0:T(4,128)(2,1)S(1)} %get-tuple-element.85), channel_id=1, source_target_pairs={{0,8},{8,16},{16,24},{24,32},{32,40},{40,48},{48,56},{56,64},{64,7... | collective-permute-start | bytes 49160 | tf_op jit(solution)/shard_map/ppermute | solution.py:16
  186.3 30.4 %collective-permute-start.3 = (bf16[4,2048]{1,0:T(4,128)(2,1)S(1)}, bf16[4,2048]{1,0:T(4,128)(2,1)S(1)}, u32[]{:S(2)}, u32[]{:S(2)}) collective-permute-start(bf16[4,2048]{1,0:T(4,128)(2,1)S(1)} %get-tuple-element.86), channel_id=1, source_target_pairs={{8,0},{16,8},{24,16},{32,24},{40,32},{48,40},{56,48},{64,56},{72,6... | collective-permute-start | bytes 49160 | tf_op jit(solution)/shard_map/ppermute | solution.py:19
  223.3 126.8 %all-gather.16.cloned.1.call-start = ((), (), s32[]{:S(2)}) async-start(), calls=%async_computation.17 | async-start | bytes 4456448 | tf_op jit(solution)/shard_map/all_gather | solution.py:166
  254.2 131.5 %all-gather.18.cloned.1.call-start = ((), (), s32[]{:S(2)}) async-start(), calls=%async_computation.18 | async-start | bytes 2359296 | tf_op jit(solution)/shard_map/all_gather | solution.py:183
  254.8 173.2 %all-gather.20.cloned.1.call-start = ((), (), s32[]{:S(2)}) async-start(), calls=%async_computation.19 | async-start | bytes 2359296 | tf_op jit(solution)/shard_map/all_gather | solution.py:184
  255.4 297.0 %reduce-scatter.15.cloned.1.call-start = ((), (), s32[]{:S(2)}) async-start(), calls=%async_computation.20 | async-start | bytes 4456448 | tf_op jit(solution)/shard_map/reduce_scatter | solution.py:233
  472.8 163.5 %reduce-scatter.17.cloned.1.call-start = ((), (), s32[]{:S(2)}) async-start(), calls=%async_computation.21 | async-start | bytes 4456448 | tf_op jit(solution)/shard_map/reduce_scatter | solution.py:239
  493.8 225.7 %reduce-scatter.19.cloned.1.call-start = ((), (), s32[]{:S(2)}) async-start(), calls=%async_computation.22 | async-start | bytes 589824 | tf_op jit(solution)/shard_map/reduce_scatter | solution.py:334
  509.1 127.2 %copy-start.60 = (bf16[512,512]{1,0:T(8,128)(2,1)S(1)}, bf16[512,512]{1,0:T(8,128)(2,1)}, u32[]{:S(2)}) copy-start(bf16[512,512]{1,0:T(8,128)(2,1)} %copy-done.59) | copy-start | bytes 1572868
  509.4 129.0 %copy-start.54 = (f32[256,512]{1,0:T(8,128)S(1)}, f32[256,512]{1,0:T(8,128)}, u32[]{:S(2)}) copy-start(f32[256,512]{1,0:T(8,128)} %copy-done.53) | copy-start | bytes 1572868
  644.6 7.0 collective-permute-start.4
  645.9 5.7 collective-permute-start.5
  665.8 6.2 collective-permute-start.6
  667.2 4.8 collective-permute-start.7
  676.5 82.0 %reduce-scatter.37.cloned.1.call-start = ((), (), s32[]{:S(2)}) async-start(), calls=%async_computation.31 | async-start | bytes 589824 | tf_op jit(solution)/shard_map/reduce_scatter | solution.py:268
  677.7 119.9 %reduce-scatter.31.cloned.1.call-start = ((), (), s32[]{:S(2)}) async-start(), calls=%async_computation.28 | async-start | bytes 589824 | tf_op jit(solution)/shard_map/reduce_scatter | solution.py:259
  678.9 162.6 %reduce-scatter.41.cloned.1.call-start = ((), (), s32[]{:S(2)}) async-start(), calls=%async_computation.33 | async-start | bytes 2359296 | tf_op jit(solution)/shard_map/reduce_scatter | solution.py:205
  682.8 202.9 %reduce-scatter.39.cloned.1.call-start = ((), (), s32[]{:S(2)}) async-start(), calls=%async_computation.32 | async-start | bytes 2359296 | tf_op jit(solution)/shard_map/reduce_scatter | solution.py:202
  686.4 237.9 %reduce-scatter.35.cloned.1.call-start = ((), (), s32[]{:S(2)}) async-start(), calls=%async_computation.30 | async-start | bytes 589824 | tf_op jit(solution)/shard_map/reduce_scatter | solution.py:265
  687.6 275.6 %reduce-scatter.33.cloned.1.call-start = ((), (), s32[]{:S(2)}) async-start(), calls=%async_computation.29 | async-start | bytes 589824 | tf_op jit(solution)/shard_map/reduce_scatter | solution.py:262
  688.9 313.9 %reduce-scatter.21.cloned.1.call-start = ((), (), s32[]{:S(2)}) async-start(), calls=%async_computation.23 | async-start | bytes 589824 | tf_op jit(solution)/shard_map/reduce_scatter | solution.py:337
  690.2 352.1 %reduce-scatter.25.cloned.1.call-start = ((), (), s32[]{:S(2)}) async-start(), calls=%async_computation.25 | async-start | bytes 884736 | tf_op jit(solution)/shard_map/reduce_scatter | solution.py:310
  691.7 391.0 %reduce-scatter.29.cloned.1.call-start = ((), (), s32[]{:S(2)}) async-start(), calls=%async_computation.27 | async-start | bytes 1179648 | tf_op jit(solution)/shard_map/reduce_scatter | solution.py:319
  694.4 432.4 %reduce-scatter.23.cloned.1.call-start = ((), (), s32[]{:S(2)}) async-start(), calls=%async_computation.24 | async-start | bytes 2359296 | tf_op jit(solution)/shard_map/reduce_scatter | solution.py:307
  696.6 468.6 %reduce-scatter.27.cloned.1.call-start = ((), (), s32[]{:S(2)}) async-start(), calls=%async_computation.26 | async-start | bytes 73728 | tf_op jit(solution)/shard_map/reduce_scatter | solution.py:316
  698.8 534.7 %all-gather.22.cloned.1.call-start = ((), (), s32[]{:S(2)}) async-start(), calls=%async_computation.34 | async-start | bytes 1114112 | tf_op jit(solution)/shard_map/all_gather | solution.py:343
  719.5 637.5 %all-reduce.17.cloned.1.call-start = ((), (), s32[]{:S(2)}) async-start(), calls=%async_computation.35 | async-start | bytes 2686976 | tf_op jit(solution)/shard_map/psum | solution.py:344
  (161 other events, 2293.4 us)
Sparse Core Ops, SparseCore 0:
  9.7 44.3 all-gather.9
  104.1 42.9 all-gather.11
  223.4 65.5 all-gather.13
  291.9 52.3 all-gather.15
  345.8 39.8 all-gather.17
  387.2 40.7 all-gather.19
  472.9 79.4 reduce-scatter.14
  556.9 79.2 reduce-scatter.16
  676.6 42.8 reduce-scatter.18
  721.8 36.6 reduce-scatter.36
  760.9 36.6 reduce-scatter.30
  800.0 41.4 reduce-scatter.40
  844.0 41.6 reduce-scatter.38
  888.0 36.1 reduce-scatter.34
  926.5 36.6 reduce-scatter.32
  966.1 36.6 reduce-scatter.20
  1005.0 37.2 reduce-scatter.24
  1044.7 37.9 reduce-scatter.28
  1085.2 41.5 reduce-scatter.22
  1129.7 35.5 reduce-scatter.26
  1167.7 43.4 all-gather.21
  1214.6 142.3 all-reduce.16
